TPU v7x, 32 devices: a whole 2x2x4 slice. The times are simulated.
32 devices in a mesh: dom: 8 (over z, y), sub: 4 (over x, core).
Axes of the slice: x: 2, y: 2, z: 4, core: 2. Of those that a mesh axis runs over, the one named last changes fastest.
Arguments:
- pair_blocks: bfloat16 [2048, 128, 128], P(('dom', 'sub')), may hold values from -0.5 to 0.5
- pair_centers: bfloat16 [2048, 2, 3, 128], P(('dom', 'sub')), may hold values from 0 to 8
- pair_expo: bfloat16 [2048, 2, 128], P(('dom', 'sub')), may hold values from 0.049804688 to 0.5
- pair_linear_terms: bfloat16 [2048, 2, 3, 128], P(('dom', 'sub')), may hold values from -0.14941406 to 0.14941406
- pair_dest: int32 [2048, 1], P(('dom', 'sub')), may hold values from 0 to 7; in each aligned block of 64 rows (0 to 63, 64 to 127, ...) at most 16 rows name the same one
- pair_tiles: int32 [2048, 2], P(('dom', 'sub')), may hold values from 0 to 31
- slab_from: int32 [32, 8], P(('dom', 'sub')), may hold values from 0 to 7, each once within a row
Outputs:
- wave_slab_density: float32 [256, 512], P(('dom', 'sub'))
Inputs may be any that keep to these rules, and one draw needn't show every extreme that they name: `pair_dest`: in the rows of one device no domain is named by more than 16 rows. `slab_from`: each row is a permutation.
All inputs are finite; a program needn't handle non-finite values.
Results may differ from a plain program's by a relative error of at most 0.0028.
Values may be sent and summed in bfloat16 or wider, within the bound.
No kernel may reach another device: no remote copies, remote signals or barrier semaphores. Data moves between devices by JAX's collectives and lax.ppermute only.
A program may use at most 64 MiB of HBM per device.

v0:
```python
import jax
import jax.numpy as jnp
from jax import lax
from jax.sharding import PartitionSpec as P

TE = 8
TPB = 2
TPD = 4


slot_group = 16


def region_points():
    tile_cells = TE**3
    index = jnp.arange(TPB * tile_cells, dtype=jnp.int32)
    coord_x = index // tile_cells * TE + index % tile_cells // (TE * TE)
    coord_y = index // TE % TE
    coord_z = index % TE
    return [coord_x.astype(jnp.float32), coord_y.astype(jnp.float32), coord_z.astype(jnp.float32)]


def basis_values(centers, expo, slope):
    points = region_points()
    stretch = [float(TPB), 1.0, 1.0]
    radius = jnp.zeros((), jnp.float32)
    linear = jnp.ones((), jnp.float32)
    for axis_index in range(3):
        middle_point = stretch[axis_index] * centers[:, :, axis_index, :].astype(jnp.float32)
        offset = points[axis_index][None, None, None, :] - middle_point[..., None]
        radius = radius + offset * offset
        linear = linear + slope[:, :, axis_index, :].astype(jnp.float32)[..., None] * offset
    return linear * jnp.exp(-expo.astype(jnp.float32)[..., None] * radius)


def group_density(block_list, centers, expo, slope):
    values = basis_values(centers, expo, slope)
    right_factor = values[:, 1].astype(jnp.bfloat16)
    pair_product = jnp.einsum(
        "pck,pka->pca", block_list, right_factor, preferred_element_type=jnp.float32
    )
    density = 2.0 * jnp.sum(values[:, 0] * pair_product, axis=1)
    return density.reshape(block_list.shape[0], TPB, TE**3)


def collocate_all(block_list, centers, expo, slope):
    group_count = block_list.shape[0] // slot_group
    width = block_list.shape[1]

    def handle(items):
        return group_density(items[0], items[1], items[2], items[3])

    density = lax.map(
        handle,
        (
            block_list.reshape(group_count, slot_group, width, width),
            centers.reshape(group_count, slot_group, 2, 3, width),
            expo.reshape(group_count, slot_group, 2, width),
            slope.reshape(group_count, slot_group, 2, 3, width),
        ),
    )
    return density.reshape(block_list.shape[0], TPB, TE**3)


def local(
    pair_blocks, pair_centers, pair_expo, pair_linear_terms, pair_dest, pair_tiles, slab_from
):
    dom_count = lax.axis_size("dom")
    sub_count = lax.axis_size("sub")
    local_blocks = pair_blocks.shape[0]
    capacity = max(2, 2 * local_blocks // dom_count)
    tile_count = dom_count * TPD
    quarter = TPD // sub_count
    targets = pair_dest[:, 0]
    one_hot = (targets[:, None] == jnp.arange(dom_count, dtype=jnp.int32)[None, :]).astype(
        jnp.int32
    )
    target_positions = jnp.sum((jnp.cumsum(one_hot, axis=0) - one_hot) * one_hot, axis=1)

    def bucket(values, filler):
        holder = jnp.full((dom_count, capacity) + values.shape[1:], filler, values.dtype)
        return holder.at[targets, target_positions].set(values)

    def flatten(values):
        return values.reshape((dom_count * capacity,) + values.shape[2:])

    partial_value = jnp.zeros((tile_count, TE**3), jnp.float32)
    arrived = (
        lax.all_to_all(bucket(pair_blocks, 0), "dom", split_axis=0, concat_axis=0, tiled=True),
        lax.all_to_all(bucket(pair_centers, 0), "dom", split_axis=0, concat_axis=0, tiled=True),
        lax.all_to_all(bucket(pair_expo, 0), "dom", split_axis=0, concat_axis=0, tiled=True),
        lax.all_to_all(
            bucket(pair_linear_terms, 0), "dom", split_axis=0, concat_axis=0, tiled=True
        ),
        lax.all_to_all(
            bucket(pair_tiles, tile_count), "dom", split_axis=0, concat_axis=0, tiled=True
        ),
    )
    density = collocate_all(
        flatten(arrived[0]), flatten(arrived[1]), flatten(arrived[2]), flatten(arrived[3])
    )
    tile_ids = flatten(arrived[4]).reshape(-1)
    partial_value = partial_value.at[tile_ids].add(density.reshape(-1, TE**3), mode="drop")
    grid_tiles = partial_value.reshape(dom_count, TPD, TE**3)
    moved = lax.all_to_all(grid_tiles, "dom", split_axis=0, concat_axis=0, tiled=True)
    summed_total = lax.psum_scatter(moved, "sub", scatter_dimension=1, tiled=True)
    flat_tiles = summed_total.reshape(dom_count * quarter, TE**3)
    return flat_tiles[slab_from[0]]


def solution(mesh):
    placed = (
        P(("dom", "sub"), None, None),
        P(("dom", "sub"), None, None, None),
        P(("dom", "sub"), None, None),
        P(("dom", "sub"), None, None, None),
        P(("dom", "sub"), None),
        P(("dom", "sub"), None),
        P(("dom", "sub"), None),
    )
    return jax.shard_map(
        local, mesh=mesh, in_specs=placed, out_specs=P(("dom", "sub"), None), check_vma=False
    )
```

profile of v0, /device:TPU:0, one launch (start us, length us, event | category | flops | bytes accessed | tf_op | source)
XLA Modules:
  0.0 332.1 jit_solution(1424790487667651080)
XLA Ops:
  9.6 3.7 %scatter_fusion = s32[8,16,2]{2,1,0:T(8,128)S(1)} fusion(s32[8,16,2]{2,1,0:T(8,128)S(1)} %broadcast_in_dim.12, s32[64]{0:T(128)S(1)} %fusion.50, s32[64,2]{1,0:T(8,128)S(1)} %copy.16), kind=kCustom, calls=%fused_computation.1 | custom fusion | bytes 2048 | tf_op jit(solution)/shard_map/scatter | solution.py:82
  14.1 7.3 %all-to-all-start = ((s32[8,16,2]{1,2,0:T(2,128)}), s32[8,16,2]{1,2,0:T(2,128)S(1)}, u32[]{:S(2)}, u32[]{:S(2)}) async-start(s32[8,16,2]{1,2,0:T(2,128)} %copy.17), calls=%async_computation | async-start | bytes 16384 | tf_op jit(solution)/shard_map/all_to_all | solution.py:95
  22.0 7.5 %scatter_fusion.3 = bf16[8,16,2,128]{3,2,1,0:T(2,128)(2,1)} fusion(bf16[8,16,2,128]{3,2,1,0:T(2,128)(2,1)} %broadcast_in_dim.14, s32[64]{0:T(128)S(1)} %fusion.50, bf16[64,2,128]{2,1,0:T(2,128)(2,1)} %param.11), kind=kCustom, calls=%fused_computation.4 | custom fusion | bytes 98816 | tf_op jit(solution)/shard_map/scatter | solution.py:82
  29.5 6.0 %all-to-all-start.3 = ((bf16[8,16,2,128]{3,2,1,0:T(2,128)(2,1)}), bf16[8,16,2,128]{3,2,1,0:T(2,128)(2,1)S(1)}, u32[]{:S(2)}, u32[]{:S(2)}) async-start(bf16[8,16,2,128]{3,2,1,0:T(2,128)(2,1)} %scatter_fusion.3), calls=%async_computation.3 | async-start | bytes 131072 | tf_op jit(solution)/shard_map/all_to_all | solution.py:91
  36.2 8.4 %scatter_fusion.1 = bf16[8,16,2,3,128]{4,2,3,1,0:T(2,128)(2,1)} fusion(bf16[8,16,2,3,128]{4,2,3,1,0:T(2,128)(2,1)} %broadcast.365.clone, s32[64]{0:T(128)S(1)} %fusion.50, bf16[64,2,3,128]{3,1,2,0:T(2,128)(2,1)} %param.12), kind=kCustom, calls=%fused_computation.2 | custom fusion | bytes 295424 | tf_op jit(solution)/shard_map/scatter | solution.py:82
  44.6 6.0 %all-to-all-start.1 = ((bf16[8,16,2,3,128]{4,2,3,1,0:T(2,128)(2,1)}), bf16[8,16,2,3,128]{4,2,3,1,0:T(2,128)(2,1)S(1)}, u32[]{:S(2)}, u32[]{:S(2)}) async-start(bf16[8,16,2,3,128]{4,2,3,1,0:T(2,128)(2,1)} %scatter_fusion.1), calls=%async_computation.1 | async-start | bytes 393216 | tf_op jit(solution)/shard_map/all_to_all | solution.py:92
  51.4 8.4 %scatter_fusion.2 = bf16[8,16,2,3,128]{4,2,3,1,0:T(2,128)(2,1)} fusion(bf16[8,16,2,3,128]{4,2,3,1,0:T(2,128)(2,1)} %broadcast.365.clone.1, s32[64]{0:T(128)S(1)} %fusion.50, bf16[64,2,3,128]{3,1,2,0:T(2,128)(2,1)} %param.10), kind=kCustom, calls=%fused_computation.3 | custom fusion | bytes 295424 | tf_op jit(solution)/shard_map/scatter | solution.py:82
  59.8 6.0 %all-to-all-start.2 = ((bf16[8,16,2,3,128]{4,2,3,1,0:T(2,128)(2,1)}), bf16[8,16,2,3,128]{4,2,3,1,0:T(2,128)(2,1)S(1)}, u32[]{:S(2)}, u32[]{:S(2)}) async-start(bf16[8,16,2,3,128]{4,2,3,1,0:T(2,128)(2,1)} %scatter_fusion.2), calls=%async_computation.2 | async-start | bytes 393216 | tf_op jit(solution)/shard_map/all_to_all | solution.py:90
  65.7 3.0 broadcast_in_dim.15
  68.8 10.7 %scatter_fusion.4 = bf16[8,16,128,128]{3,2,1,0:T(8,128)(2,1)} fusion(bf16[8,16,128,128]{3,2,1,0:T(8,128)(2,1)} %broadcast_in_dim.15, s32[64]{0:T(128)S(1)} %fusion.50, bf16[64,128,128]{2,1,0:T(8,128)(2,1)} %param.9), kind=kCustom, calls=%fused_computation.5 | custom fusion | bytes 6291968 | tf_op jit(solution)/shard_map/scatter | solution.py:82
  79.4 6.0 %all-to-all-start.4 = ((bf16[8,16,128,128]{3,2,1,0:T(8,128)(2,1)}), bf16[8,16,128,128]{3,2,1,0:T(8,128)(2,1)}, u32[]{:S(2)}, u32[]{:S(2)}) async-start(bf16[8,16,128,128]{3,2,1,0:T(8,128)(2,1)} %scatter_fusion.4), calls=%async_computation.4 | async-start | bytes 8388608 | tf_op jit(solution)/shard_map/all_to_all | solution.py:89
  85.8 90.8 %all-to-all-done.4 = bf16[8,16,128,128]{3,2,1,0:T(8,128)(2,1)} async-done(((bf16[8,16,128,128]{3,2,1,0:T(8,128)(2,1)}), bf16[8,16,128,128]{3,2,1,0:T(8,128)(2,1)}, u32[]{:S(2)}, u32[]{:S(2)}) %all-to-all-start.4) | async-done | bytes 4194336 | tf_op jit(solution)/shard_map/all_to_all | solution.py:89
  176.6 116.2 %while.13 = (s32[]{:T(128)}, f32[8,16,2,512]{3,2,1,0:T(2,128)S(1)}, bf16[8,16,2,3,128]{4,2,3,1,0:T(2,128)(2,1)S(1)}, bf16[8,16,2,3,128]{4,2,3,1,0:T(2,128)(2,1)S...) while((s32[]{:T(128)}, f32[8,16,2,512]{3,2,1,0:T(2,128)S(1)}, ...), condition=%wide.region_9.10_spmd, body=%wide.region_7.9_spmd.sunk | while | flops 610364416 | bytes 35062360 | solution.py:53
  176.7 11.7 %fusion.65 = f32[16,2,128,1024]{3,2,0,1:T(8,128)S(1)} fusion(f32[16,2,128]{2,0,1:T(8,128)S(1)} %negate_bitcast_fusion.2, f32[16,2,128]{2,0,1:T(8,128)S(1)} %get-tuple-element.207, f32[1024]{0:T(1024)S(1)} %fusion.62, f32[16,2,128]{2,0,1:T(8,128)S(1)} %get-tuple-element.209, f32[16,2,128]{2,0,1:T(8,128)S(1)} %get-tuple-element.210, ...), kind=kLoop, calls=%fused_computation.16.clone.1 | loop fusion | flops 67108864 | bytes 16904192 | tf_op jit(solution)/shard_map/while/body/eval_jaxpr/mul | solution.py:33
  188.5 2.5 fusion.66
  191.3 11.7 %fusion.65 = f32[16,2,128,1024]{3,2,0,1:T(8,128)S(1)} fusion(f32[16,2,128]{2,0,1:T(8,128)S(1)} %negate_bitcast_fusion.2, f32[16,2,128]{2,0,1:T(8,128)S(1)} %get-tuple-element.207, f32[1024]{0:T(1024)S(1)} %fusion.62, f32[16,2,128]{2,0,1:T(8,128)S(1)} %get-tuple-element.209, f32[16,2,128]{2,0,1:T(8,128)S(1)} %get-tuple-element.210, ...), kind=kLoop, calls=%fused_computation.16.clone.1 | loop fusion | flops 67108864 | bytes 16904192 | tf_op jit(solution)/shard_map/while/body/eval_jaxpr/mul | solution.py:33
  203.0 2.5 fusion.66
  205.8 11.7 %fusion.65 = f32[16,2,128,1024]{3,2,0,1:T(8,128)S(1)} fusion(f32[16,2,128]{2,0,1:T(8,128)S(1)} %negate_bitcast_fusion.2, f32[16,2,128]{2,0,1:T(8,128)S(1)} %get-tuple-element.207, f32[1024]{0:T(1024)S(1)} %fusion.62, f32[16,2,128]{2,0,1:T(8,128)S(1)} %get-tuple-element.209, f32[16,2,128]{2,0,1:T(8,128)S(1)} %get-tuple-element.210, ...), kind=kLoop, calls=%fused_computation.16.clone.1 | loop fusion | flops 67108864 | bytes 16904192 | tf_op jit(solution)/shard_map/while/body/eval_jaxpr/mul | solution.py:33
  217.5 2.5 fusion.66
  220.3 11.7 %fusion.65 = f32[16,2,128,1024]{3,2,0,1:T(8,128)S(1)} fusion(f32[16,2,128]{2,0,1:T(8,128)S(1)} %negate_bitcast_fusion.2, f32[16,2,128]{2,0,1:T(8,128)S(1)} %get-tuple-element.207, f32[1024]{0:T(1024)S(1)} %fusion.62, f32[16,2,128]{2,0,1:T(8,128)S(1)} %get-tuple-element.209, f32[16,2,128]{2,0,1:T(8,128)S(1)} %get-tuple-element.210, ...), kind=kLoop, calls=%fused_computation.16.clone.1 | loop fusion | flops 67108864 | bytes 16904192 | tf_op jit(solution)/shard_map/while/body/eval_jaxpr/mul | solution.py:33
  232.0 2.5 fusion.66
  234.8 11.7 %fusion.65 = f32[16,2,128,1024]{3,2,0,1:T(8,128)S(1)} fusion(f32[16,2,128]{2,0,1:T(8,128)S(1)} %negate_bitcast_fusion.2, f32[16,2,128]{2,0,1:T(8,128)S(1)} %get-tuple-element.207, f32[1024]{0:T(1024)S(1)} %fusion.62, f32[16,2,128]{2,0,1:T(8,128)S(1)} %get-tuple-element.209, f32[16,2,128]{2,0,1:T(8,128)S(1)} %get-tuple-element.210, ...), kind=kLoop, calls=%fused_computation.16.clone.1 | loop fusion | flops 67108864 | bytes 16904192 | tf_op jit(solution)/shard_map/while/body/eval_jaxpr/mul | solution.py:33
  246.6 2.5 fusion.66
  249.4 11.7 %fusion.65 = f32[16,2,128,1024]{3,2,0,1:T(8,128)S(1)} fusion(f32[16,2,128]{2,0,1:T(8,128)S(1)} %negate_bitcast_fusion.2, f32[16,2,128]{2,0,1:T(8,128)S(1)} %get-tuple-element.207, f32[1024]{0:T(1024)S(1)} %fusion.62, f32[16,2,128]{2,0,1:T(8,128)S(1)} %get-tuple-element.209, f32[16,2,128]{2,0,1:T(8,128)S(1)} %get-tuple-element.210, ...), kind=kLoop, calls=%fused_computation.16.clone.1 | loop fusion | flops 67108864 | bytes 16904192 | tf_op jit(solution)/shard_map/while/body/eval_jaxpr/mul | solution.py:33
  261.1 2.5 fusion.66
  263.9 11.7 %fusion.65 = f32[16,2,128,1024]{3,2,0,1:T(8,128)S(1)} fusion(f32[16,2,128]{2,0,1:T(8,128)S(1)} %negate_bitcast_fusion.2, f32[16,2,128]{2,0,1:T(8,128)S(1)} %get-tuple-element.207, f32[1024]{0:T(1024)S(1)} %fusion.62, f32[16,2,128]{2,0,1:T(8,128)S(1)} %get-tuple-element.209, f32[16,2,128]{2,0,1:T(8,128)S(1)} %get-tuple-element.210, ...), kind=kLoop, calls=%fused_computation.16.clone.1 | loop fusion | flops 67108864 | bytes 16904192 | tf_op jit(solution)/shard_map/while/body/eval_jaxpr/mul | solution.py:33
  275.6 2.5 fusion.66
  278.4 11.7 %fusion.65 = f32[16,2,128,1024]{3,2,0,1:T(8,128)S(1)} fusion(f32[16,2,128]{2,0,1:T(8,128)S(1)} %negate_bitcast_fusion.2, f32[16,2,128]{2,0,1:T(8,128)S(1)} %get-tuple-element.207, f32[1024]{0:T(1024)S(1)} %fusion.62, f32[16,2,128]{2,0,1:T(8,128)S(1)} %get-tuple-element.209, f32[16,2,128]{2,0,1:T(8,128)S(1)} %get-tuple-element.210, ...), kind=kLoop, calls=%fused_computation.16.clone.1 | loop fusion | flops 67108864 | bytes 16904192 | tf_op jit(solution)/shard_map/while/body/eval_jaxpr/mul | solution.py:33
  290.1 2.5 fusion.66
  293.1 2.1 scatter_custom_fusion.5
  295.2 10.3 %all_to_all.30 = f32[8,4,512]{2,1,0:T(4,128)S(1)} all-to-all(f32[8,4,512]{2,1,0:T(4,128)S(1)} %reshape.242), channel_id=1, replica_groups=mesh['dom'=8,'sub'=4] {'dom'}, dimensions={0} | all-to-all | bytes 131072 | tf_op jit(solution)/shard_map/all_to_all | solution.py:105
  306.3 17.1 %reduce-scatter.2.cloned.1.call-done = f32[8,1,512]{2,0,1:T(8,128)} async-done(((f32[8,4,512]{2,0,1:T(8,128)}), f32[8,1,512]{2,0,1:T(8,128)}) %reduce-scatter.2.cloned.1.call-update) | async-done | bytes 16400 | tf_op jit(solution)/shard_map/reduce_scatter | solution.py:106
  (132 shorter events, 10.8 us)
Async XLA Ops:
  14.1 15.4 %all-to-all-start = ((s32[8,16,2]{1,2,0:T(2,128)}), s32[8,16,2]{1,2,0:T(2,128)S(1)}, u32[]{:S(2)}, u32[]{:S(2)}) async-start(s32[8,16,2]{1,2,0:T(2,128)} %copy.17), calls=%async_computation | async-start | bytes 16384 | tf_op jit(solution)/shard_map/all_to_all | solution.py:95
  29.5 15.1 %all-to-all-start.3 = ((bf16[8,16,2,128]{3,2,1,0:T(2,128)(2,1)}), bf16[8,16,2,128]{3,2,1,0:T(2,128)(2,1)S(1)}, u32[]{:S(2)}, u32[]{:S(2)}) async-start(bf16[8,16,2,128]{3,2,1,0:T(2,128)(2,1)} %scatter_fusion.3), calls=%async_computation.3 | async-start | bytes 131072 | tf_op jit(solution)/shard_map/all_to_all | solution.py:91
  44.6 15.1 %all-to-all-start.1 = ((bf16[8,16,2,3,128]{4,2,3,1,0:T(2,128)(2,1)}), bf16[8,16,2,3,128]{4,2,3,1,0:T(2,128)(2,1)S(1)}, u32[]{:S(2)}, u32[]{:S(2)}) async-start(bf16[8,16,2,3,128]{4,2,3,1,0:T(2,128)(2,1)} %scatter_fusion.1), calls=%async_computation.1 | async-start | bytes 393216 | tf_op jit(solution)/shard_map/all_to_all | solution.py:92
  59.8 19.7 %all-to-all-start.2 = ((bf16[8,16,2,3,128]{4,2,3,1,0:T(2,128)(2,1)}), bf16[8,16,2,3,128]{4,2,3,1,0:T(2,128)(2,1)S(1)}, u32[]{:S(2)}, u32[]{:S(2)}) async-start(bf16[8,16,2,3,128]{4,2,3,1,0:T(2,128)(2,1)} %scatter_fusion.2), calls=%async_computation.2 | async-start | bytes 393216 | tf_op jit(solution)/shard_map/all_to_all | solution.py:90
  79.4 97.1 %all-to-all-start.4 = ((bf16[8,16,128,128]{3,2,1,0:T(8,128)(2,1)}), bf16[8,16,128,128]{3,2,1,0:T(8,128)(2,1)}, u32[]{:S(2)}, u32[]{:S(2)}) async-start(bf16[8,16,128,128]{3,2,1,0:T(8,128)(2,1)} %scatter_fusion.4), calls=%async_computation.4 | async-start | bytes 8388608 | tf_op jit(solution)/shard_map/all_to_all | solution.py:89
  85.4 238.0 %reduce-scatter.2.cloned.1.call-start = ((), (), s32[]{:S(2)}) async-start(), calls=%async_computation.7 | async-start | bytes 81920 | tf_op jit(solution)/shard_map/reduce_scatter | solution.py:106
  176.6 129.7 %copy-start = (s32[1,8]{1,0:T(1,128)S(1)}, s32[1,8]{1,0:T(1,128)}, u32[]{:S(2)}) copy-start(s32[1,8]{1,0:T(1,128)} %param.15) | copy-start | bytes 100
Sparse Core Ops, SparseCore 0:
  306.4 16.9 reduce-scatter.1
where the time goes:
time: 334 us; the launch traced here: 332 us
  waiting for transfers between devices  108 us (32%)
  other arithmetic  98.6 us (30%)
  local copies, waits for them, and re-layouts  49.7 us (15%)
  starting transfers between devices  31.2 us (9%)
  matrix products  19.9 us (6%)
  between operations  13.5 us (4%)
  blocking collectives  10.3 us (3%)
    mul x8, other arithmetic, basis_values(): return linear * jnp.exp(-expo.astype(jnp.float32)[..., None] * radius)  93.8 us
    all_to_all x1, waiting for transfers between devices, local(): lax.all_to_all(bucket(pair_blocks, 0), 'dom', split_axis=0, concat_axis=0...  90.8 us
    scatter x6, local copies, waits for them, and re-layouts, bucket(): return holder.at[targets, target_positions].set(values)  39.4 us
    dot_general x8, matrix products, group_density(): jnp.einsum('pck,pka->pca', block_list, right_factor, preferred_element_ty...  19.9 us
    reduce_scatter x1, waiting for transfers between devices, local(): lax.psum_scatter(moved, 'sub', scatter_dimension=1, tiled=True)  17.1 us
    all_to_all x1, blocking collectives, local(): lax.all_to_all(grid_tiles, 'dom', split_axis=0, concat_axis=0, tiled=True)  10.3 us
    all_to_all x1, starting transfers between devices, local(): lax.all_to_all(bucket(pair_tiles, tile_count), 'dom', split_axis=0, conca...  7.27 us
  transfers between devices with their start and end apart: 6, of which 2 were waited for; matrix products, arithmetic and copies ran while one was open for 12% of the time, Pallas kernels for 0%

commit v1 on v0

v1 whole, which is shorter than its diff:
```python
import functools

import jax
import jax.numpy as jnp
from jax import lax
from jax.experimental import pallas as pl
from jax.experimental.pallas import tpu as pltpu
from jax.sharding import PartitionSpec as P

TE = 8
TPB = 2
TPD = 4
CELLS = TE**3
PLANE = TE * TE
AXES = ("dom", "sub")
STEP_BLOCKS = 8
DENSE_ROWS = 1024


def side_factors(center, expo, slope):
    width = expo.shape[-1]

    def steps(count):
        return lax.broadcasted_iota(jnp.int32, (count, width), 0).astype(jnp.float32)

    ux = steps(TPB * TE) - float(TPB) * center[0]
    uy = steps(TE) - center[1]
    uz = steps(TE) - center[2]
    ex = jnp.exp(-expo * (ux * ux))
    ey = jnp.exp(-expo * (uy * uy))
    ez = jnp.exp(-expo * (uz * uz))
    yz = ey[:, None, :] * ez[None]
    head = (1.0 - slope[0] * (float(TPB) * center[0])) + slope[1] * uy
    t = yz * (head[:, None, :] + (slope[2] * uz)[None])
    d = yz * slope[0][None]
    return ex, t, d


def density_kernel(
    blocks_ref, center_ref, expo_ref, slope_ref, row_ref, out_ref, weight, column, scaled, spread, total
):
    step = pl.program_id(0)
    count, width = blocks_ref.shape[0], blocks_ref.shape[1]
    row_count = out_ref.shape[0]

    @pl.when(step == 0)
    def _():
        weight[...] = jnp.zeros_like(weight)
        total[...] = jnp.zeros_like(total)

    def factors(i, which):
        center = center_ref[i].astype(jnp.float32)
        expo = expo_ref[i].astype(jnp.float32)
        slope = slope_ref[i].astype(jnp.float32)
        return side_factors(
            [center[which, a : a + 1] for a in range(3)],
            expo[which : which + 1],
            [slope[which, a : a + 1] for a in range(3)],
        )

    rows = row_ref[...]
    lanes = lax.broadcasted_iota(jnp.int32, (count, row_count), 1)
    hot = [jnp.where(rows[:, k : k + 1] == lanes, 2.0, 0.0) for k in range(TPB)]
    for pair in range(count // 2):
        for h in range(2):
            i = 2 * pair + h
            own = slice(h * width, (h + 1) * width)
            weight[pair, own, own] = blocks_ref[i]
            ex, t, d = factors(i, 1)
            for x in range(TPB * TE):
                value = (t * ex[x : x + 1][None]).reshape(PLANE, width)
                column[pair, x * PLANE : (x + 1) * PLANE, own] = value.astype(jnp.bfloat16)
                t = t + d
            for k in range(TPB):
                slot = (TPB * i + k) * width
                spread[slot : slot + width, :] = jnp.broadcast_to(
                    hot[k][i : i + 1], (width, row_count)
                ).astype(jnp.bfloat16)
        product = lax.dot_general(
            column[pair], weight[pair], (((1,), (1,)), ((), ())), preferred_element_type=jnp.float32
        )
        for h in range(2):
            i = 2 * pair + h
            ex, t, d = factors(i, 0)
            for x in range(TPB * TE):
                part = product[x * PLANE : (x + 1) * PLANE, h * width : (h + 1) * width]
                value = (t * ex[x : x + 1][None]).reshape(PLANE, width) * part
                k, q = x // TE, x % TE
                slot = (TPB * i + k) * width
                scaled[q * PLANE : (q + 1) * PLANE, slot : slot + width] = value.astype(jnp.bfloat16)
                t = t + d
    total[...] += jnp.dot(scaled[...], spread[...], preferred_element_type=jnp.float32)

    @pl.when(step == pl.num_programs(0) - 1)
    def _():
        out_ref[...] = total[...].T.astype(out_ref.dtype)


def tile_sums(blocks, center, expo, slope, rows, row_count, out_type):
    number, width = blocks.shape[0], blocks.shape[1]
    per_step = STEP_BLOCKS

    def split(*rest):
        return pl.BlockSpec((per_step,) + rest, lambda g: (g,) + (0,) * len(rest))

    return pl.pallas_call(
        density_kernel,
        grid=(number // per_step,),
        in_specs=[
            split(width, width),
            split(2, 3, width),
            split(2, width),
            split(2, 3, width),
            split(TPB),
        ],
        out_specs=pl.BlockSpec((row_count, CELLS), lambda g: (0, 0)),
        out_shape=jax.ShapeDtypeStruct((row_count, CELLS), out_type),
        scratch_shapes=[
            pltpu.VMEM((per_step // 2, 2 * width, 2 * width), jnp.bfloat16),
            pltpu.VMEM((per_step // 2, TPB * CELLS, 2 * width), jnp.bfloat16),
            pltpu.VMEM((CELLS, per_step * TPB * width), jnp.bfloat16),
            pltpu.VMEM((per_step * TPB * width, row_count), jnp.bfloat16),
            pltpu.VMEM((CELLS, row_count), jnp.float32),
        ],
        compiler_params=pltpu.CompilerParams(vmem_limit_bytes=48 << 20),
    )(blocks, center, expo, slope, rows)


def pick_rows(summed, order):
    match = order[:, None] == jnp.arange(summed.shape[0], dtype=jnp.int32)[None, :]
    return jnp.sum(jnp.where(match[:, :, None], summed[None], 0.0), axis=1)


def dense_plan(blocks, center, expo, slope, dest, tiles, order, dom_count, sub_count):
    quarter = TPD // sub_count
    held = dom_count * quarter
    rows = tiles // quarter * held + dest * quarter + tiles % quarter
    partial = tile_sums(
        blocks, center, expo, slope, rows, dom_count * sub_count * held, jnp.bfloat16
    )
    moved = lax.all_to_all(
        partial.reshape(dom_count * sub_count, held, CELLS), AXES, split_axis=0, concat_axis=0, tiled=True
    )
    return pick_rows(jnp.sum(moved.astype(jnp.float32), axis=0), order)


def routed_plan(blocks, center, expo, slope, dest, tiles, order, dom_count, sub_count):
    number = blocks.shape[0]
    capacity = max(2, 2 * number // dom_count)
    tile_count = dom_count * TPD
    quarter = TPD // sub_count
    own_rows = jnp.arange(TPB * number, dtype=jnp.int32).reshape(number, TPB)
    density = tile_sums(blocks, center, expo, slope, own_rows, TPB * number, jnp.float32)
    density = density.reshape(number, TPB, CELLS).astype(jnp.bfloat16)
    targets = dest[:, 0]
    one_hot = (targets[:, None] == jnp.arange(dom_count, dtype=jnp.int32)[None, :]).astype(jnp.int32)
    places = jnp.sum((jnp.cumsum(one_hot, axis=0) - one_hot) * one_hot, axis=1)

    def exchange(values, filler):
        holder = jnp.full((dom_count, capacity) + values.shape[1:], filler, values.dtype)
        holder = holder.at[targets, places].set(values)
        return lax.all_to_all(holder, "dom", split_axis=0, concat_axis=0, tiled=True)

    arrived = exchange(density, 0).reshape(-1, CELLS).astype(jnp.float32)
    tile_ids = exchange(tiles, tile_count).reshape(-1)
    partial = jnp.zeros((tile_count, CELLS), jnp.float32).at[tile_ids].add(arrived, mode="drop")
    moved = lax.all_to_all(
        partial.reshape(dom_count, TPD, CELLS), "dom", split_axis=0, concat_axis=0, tiled=True
    )
    summed = lax.psum_scatter(moved, "sub", scatter_dimension=1, tiled=True)
    return summed.reshape(dom_count * quarter, CELLS)[order]


def local(blocks, center, expo, slope, dest, tiles, slab_from):
    dom_count, sub_count = lax.axis_size("dom"), lax.axis_size("sub")
    all_rows = dom_count * dom_count * TPD
    plan = dense_plan if all_rows <= DENSE_ROWS else routed_plan
    return plan(blocks, center, expo, slope, dest, tiles, slab_from[0], dom_count, sub_count)


def solution(mesh):
    def placed(rank):
        return P(AXES, *([None] * (rank - 1)))

    return jax.shard_map(
        local,
        mesh=mesh,
        in_specs=tuple(placed(rank) for rank in (3, 4, 3, 4, 2, 2, 2)),
        out_specs=placed(2),
        check_vma=False,
    )
```

time: 334 us -> 42.8 us (0.13)
  waiting for transfers between devices: 108 us -> 10.5 us
  other arithmetic: 98.6 us -> 2.25 us
  local copies, waits for them, and re-layouts: 49.7 us -> 4.34 us
  starting transfers between devices: 31.2 us -> 7.29 us
  matrix products: 19.9 us -> 0 us
  Pallas kernels: 0 us -> 18.1 us
  between operations: 13.5 us -> 0.03 us
  blocking collectives: 10.3 us -> 0 us
    mul x24 -> x1, other arithmetic: 93.9 us -> 0.68 us  [dense_plan(): rows = tiles // quarter * held + dest * quarter + tiles % quarter]
    all_to_all x5 -> x1, waiting for transfers between devices: 90.8 us -> 10.5 us  [dense_plan(): lax.all_to_all(partial.reshape(dom_count * sub_count, held, CELLS), AXES,...]
    scatter x6 -> x0, local copies, waits for them, and re-layouts: 39.4 us -> none  [bucket(): return holder.at[targets, target_positions].set(values)]
    all_to_all x5 -> x1, starting transfers between devices: 31.2 us -> 7.29 us  [dense_plan(): lax.all_to_all(partial.reshape(dom_count * sub_count, held, CELLS), AXES,...]
    dot_general x8 -> x0, matrix products: 19.9 us -> none  [group_density(): jnp.einsum('pck,pka->pca', block_list, right_factor, preferred_element_ty...]
    pallas_call x0 -> x1, Pallas kernels: none -> 18.1 us  [tile_sums(): pl.pallas_call(density_kernel, grid=(number // per_step,), in_specs=[spli...]
    reduce_scatter x1 -> x0, waiting for transfers between devices: 17.1 us -> none  [local(): lax.psum_scatter(moved, 'sub', scatter_dimension=1, tiled=True)]
    all_to_all x1 -> x0, blocking collectives: 10.3 us -> none  [local(): lax.all_to_all(grid_tiles, 'dom', split_axis=0, concat_axis=0, tiled=True)]
  transfers between devices with their start and end apart: 6 -> 1, of which waited for: 2 -> 1; matrix products, arithmetic and copies ran while one was open for 12% -> 0% of each run, Pallas kernels for 0% -> 0%
where the time goes in v1:
time: 42.8 us; the launch traced here: 42.5 us
  Pallas kernels  18.1 us (42%)
  waiting for transfers between devices  10.5 us (25%)
  starting transfers between devices  7.29 us (17%)
  local copies, waits for them, and re-layouts  4.34 us (10%)
  other arithmetic  2.25 us (5%)
    pallas_call x1, Pallas kernels, tile_sums(): pl.pallas_call(density_kernel, grid=(number // per_step,), in_specs=[spli...  18.1 us
    all_to_all x1, waiting for transfers between devices, dense_plan(): lax.all_to_all(partial.reshape(dom_count * sub_count, held, CELLS), AXES,...  10.5 us
    all_to_all x1, starting transfers between devices, dense_plan(): lax.all_to_all(partial.reshape(dom_count * sub_count, held, CELLS), AXES,...  7.29 us
    unnamed x8, local copies, waits for them, and re-layouts  4.24 us
  transfers between devices with their start and end apart: 1, of which 1 were waited for; matrix products, arithmetic and copies ran while one was open for 0% of the time, Pallas kernels for 0%

profile of v1, /device:TPU:0, one launch (start us, length us, event | category | flops | bytes accessed | tf_op | source)
XLA Modules:
  0.0 42.5 jit_solution(4656049281287922083)
XLA Ops:
  0.0 0.0 copy-start.2
  0.0 0.9 %copy.18.center_ref = bf16[64,2,3,128]{3,2,1,0:T(4,128)(2,1)S(1)} copy(bf16[64,2,3,128]{3,1,2,0:T(2,128)(2,1)} %param.8) | data formatting | bytes 196608 | tf_op args[1]
  1.0 0.9 %copy.19.slope_ref = bf16[64,2,3,128]{3,2,1,0:T(4,128)(2,1)S(1)} copy(bf16[64,2,3,128]{3,1,2,0:T(2,128)(2,1)} %param.10) | data formatting | bytes 196608 | tf_op args[3]
  1.9 0.7 %broadcast_multiply_fusion = s32[64,2]{0,1:T(2,128)S(1)} fusion(s32[64,2]{0,1:T(2,128)} %param.12), kind=kLoop, calls=%fused_computation.4 | loop fusion | flops 128 | bytes 1024 | tf_op jit(solution)/shard_map/mul | solution.py:137
  2.6 0.1 copy.16
  2.7 0.7 %broadcast_add_fusion.row_ref = s32[64,2]{1,0:T(8,128)S(1)} fusion(s32[64,2]{1,0:T(8,128)S(1)} %copy.16, s32[64]{0:T(128)} %bitcast.3), kind=kLoop, calls=%fused_computation.2 | loop fusion | flops 128 | bytes 1280 | tf_op jit(solution)/shard_map/add | solution.py:137
  3.4 0.0 copy-start
  3.4 1.6 %copy-done = bf16[64,128,128]{2,1,0:T(8,128)(2,1)S(1)} copy-done((bf16[64,128,128]{2,1,0:T(8,128)(2,1)S(1)}, bf16[64,128,128]{2,1,0:T(8,128)(2,1)}, u32[]{:S(2)}) %copy-start) | copy-done | bytes 2097176
  5.0 0.0 copy-start.1
  5.0 0.8 %copy-done.1 = bf16[64,2,128]{2,1,0:T(2,128)(2,1)S(1)} copy-done((bf16[64,2,128]{2,1,0:T(2,128)(2,1)S(1)}, bf16[64,2,128]{2,1,0:T(2,128)(2,1)}, u32[]{:S(2)}) %copy-start.1) | copy-done | bytes 32792
  5.8 18.1 %shard_map.73 = bf16[256,512]{1,0:T(8,128)(2,1)} custom-call(bf16[64,128,128]{2,1,0:T(8,128)(2,1)S(1)} %copy-done, bf16[64,2,3,128]{3,2,1,0:T(4,128)(2,1)S(1)} %copy.18.center_ref, bf16[64,2,128]{2,1,0:T(2,128)(2,1)S(1)} %copy-done.1, bf16[64,2,3,128]{3,2,1,0:T(4,128)(2,1)S(1)} %copy.19.slope_ref, s32[64,2]{1,0:T(8,128)S(1)} %broadcast_add_fusion.row_ref), custom_call_target="tpu_custom_call" | custom-call | tf_op jit(solution)/shard_map/pallas_call | solution.py:106
  23.8 7.3 %all-to-all-start = ((bf16[32,8,512]{2,1,0:T(8,128)(2,1)}), bf16[32,8,512]{2,1,0:T(8,128)(2,1)S(1)}, u32[]{:S(2)}, u32[]{:S(2)}) async-start(bf16[32,8,512]{2,1,0:T(8,128)(2,1)} %bitcast.2), calls=%async_computation | async-start | bytes 524288 | tf_op jit(solution)/shard_map/all_to_all | solution.py:141
  31.1 0.0 copy-done.2
  31.1 0.1 iota_compare_fusion
  31.2 10.5 %all-to-all-done = bf16[32,8,512]{2,1,0:T(8,128)(2,1)S(1)} async-done(((bf16[32,8,512]{2,1,0:T(8,128)(2,1)}), bf16[32,8,512]{2,1,0:T(8,128)(2,1)S(1)}, u32[]{:S(2)}, u32[]{:S(2)}) %all-to-all-start) | async-done | bytes 262176 | tf_op jit(solution)/shard_map/all_to_all | solution.py:141
  41.8 0.7 %select_reduce_fusion = f32[8,512]{1,0:T(8,128)} fusion(f32[8,512]{1,0:T(8,128)S(1)} %convert_reduce_fusion, pred[8,8]{1,0:T(8,128)(4,1)S(1)} %iota_compare_fusion), kind=kLoop, calls=%fused_computation.1 | loop fusion | flops 61440 | bytes 32832 | tf_op jit(solution)/shard_map/reduce_sum | solution.py:131
  (1 shorter events, 0.0 us)
Async XLA Ops:
  0.0 31.1 %copy-start.2 = (s32[1,8]{1,0:T(1,128)S(1)}, s32[1,8]{1,0:T(1,128)}, u32[]{:S(2)}) copy-start(s32[1,8]{1,0:T(1,128)} %param.13) | copy-start | bytes 100
  3.4 1.6 %copy-start = (bf16[64,128,128]{2,1,0:T(8,128)(2,1)S(1)}, bf16[64,128,128]{2,1,0:T(8,128)(2,1)}, u32[]{:S(2)}) copy-start(bf16[64,128,128]{2,1,0:T(8,128)(2,1)} %blocks_ref.1) | copy-start | bytes 6291460
  5.0 0.8 %copy-start.1 = (bf16[64,2,128]{2,1,0:T(2,128)(2,1)S(1)}, bf16[64,2,128]{2,1,0:T(2,128)(2,1)}, u32[]{:S(2)}) copy-start(bf16[64,2,128]{2,1,0:T(2,128)(2,1)} %expo_ref.1) | copy-start | bytes 98308
  23.8 17.9 %all-to-all-start = ((bf16[32,8,512]{2,1,0:T(8,128)(2,1)}), bf16[32,8,512]{2,1,0:T(8,128)(2,1)S(1)}, u32[]{:S(2)}, u32[]{:S(2)}) async-start(bf16[32,8,512]{2,1,0:T(8,128)(2,1)} %bitcast.2), calls=%async_computation | async-start | bytes 524288 | tf_op jit(solution)/shard_map/all_to_all | solution.py:141

commit v2 on v1

v2 whole, which is shorter than its diff:
```python
import functools

import jax
import jax.numpy as jnp
from jax import lax
from jax.experimental import pallas as pl
from jax.experimental.pallas import tpu as pltpu
from jax.sharding import PartitionSpec as P

TE = 8
TPB = 2
TPD = 4
CELLS = TE**3
PLANE = TE * TE
AXES = ("dom", "sub")
STEP_BLOCKS = 16
LOG2_E = 1.4426950408889634
DENSE_ROWS = 1024


def side_factors(center, expo, slope, table):
    width = expo.shape[-1]
    steps = lax.broadcasted_iota(jnp.int32, (TE, width), 0).astype(jnp.float32)
    center_x = float(TPB) * center[0]
    rate = expo * (-LOG2_E)
    uy = steps - center[1]
    uz = steps - center[2]
    for k in range(TPB):
        ux = (steps + float(k * TE)) - center_x
        table[k * TE : (k + 1) * TE, :] = jnp.exp2(rate * (ux * ux))
    y_rows, slope_rows = TPB * TE, (TPB + 1) * TE
    table[y_rows : y_rows + TE, :] = jnp.exp2(rate * (uy * uy))
    table[slope_rows : slope_rows + TE, :] = (1.0 - slope[0] * center_x) + slope[1] * uy
    ez = jnp.exp2(rate * (uz * uz))
    z_part = slope[2] * uz

    def row(index):
        return jnp.broadcast_to(table[index : index + 1, :], (TE, width))

    yz = [row(y_rows + y) * ez for y in range(TE)]
    t = jnp.stack([yz[y] * (row(slope_rows + y) + z_part) for y in range(TE)])
    d = jnp.stack([value * slope[0] for value in yz])
    return row, t, d


def density_kernel(
    dest_ref,
    tile_ref,
    blocks_ref,
    center_ref,
    expo_ref,
    slope_ref,
    out_ref,
    weight,
    total,
    centers,
    expos,
    slopes,
    tables,
    *columns,
    row_of,
):
    step = pl.program_id(0)
    count, width = blocks_ref.shape[0], blocks_ref.shape[1]
    cell_rows = 4 * PLANE

    @pl.when(step == 0)
    def _():
        weight[...] = jnp.zeros_like(weight)
        total[...] = jnp.zeros_like(total)
        centers[...] = center_ref[...].astype(jnp.float32)
        expos[...] = expo_ref[...].astype(jnp.float32)
        slopes[...] = slope_ref[...].astype(jnp.float32)

    def factors(block, which, slot):
        def spread(ref, index):
            return jnp.broadcast_to(ref[pl.ds(index, 1), :], (TE, width))

        return side_factors(
            [spread(centers, 6 * block + 2 * a + which) for a in range(3)],
            spread(expos, 2 * block + which),
            [spread(slopes, 6 * block + 2 * a + which) for a in range(3)],
            tables.at[slot],
        )

    pick = lax.broadcasted_iota(jnp.int32, (16, 2 * width), 1) // width
    pick = (pick == lax.broadcasted_iota(jnp.int32, (16, 2 * width), 0)).astype(jnp.float32)
    pick = pick.astype(jnp.bfloat16)
    transposed = (((1,), (1,)), ((), ()))
    half_points = TPB * CELLS // 2

    for pair in range(count // 2):
        column = columns[pair]
        first = step * count + 2 * pair
        for h in range(2):
            own = slice(h * width, (h + 1) * width)
            weight[pair, own, own] = blocks_ref[2 * pair + h]
            row, t, d = factors(first + h, 1, 4 * pair + h)
            for x in range(TPB * TE):
                value = (t * row(x)[None]).reshape(PLANE, width)
                column[x * PLANE : (x + 1) * PLANE, own] = value.astype(jnp.bfloat16)
                t = t + d
        sides = [list(factors(first + h, 0, 4 * pair + 2 + h)) for h in range(2)]
        for half in range(2):
            product = lax.dot_general(
                column[half * half_points : (half + 1) * half_points, :],
                weight[pair],
                transposed,
                preferred_element_type=jnp.float32,
            )
            for part in range(half_points // cell_rows):
                scaled = []
                for h in range(2):
                    row, t, d = sides[h]
                    planes = []
                    for plane in range(4):
                        at = part * cell_rows + plane * PLANE
                        x = half * (half_points // PLANE) + part * 4 + plane
                        value = (t * row(x)[None]).reshape(PLANE, width)
                        value = value * product[at : at + PLANE, h * width : (h + 1) * width]
                        planes.append(value.astype(jnp.bfloat16))
                        t = t + d
                    sides[h][1] = t
                    scaled.append(jnp.concatenate(planes, axis=0))
                sums = lax.dot_general(
                    pick,
                    jnp.concatenate(scaled, axis=1),
                    transposed,
                    preferred_element_type=jnp.float32,
                )
                start = half * half_points + part * cell_rows
                k, q = start // CELLS, start % CELLS
                for h in range(2):
                    where = row_of(dest_ref, tile_ref, first + h, k)
                    total[pl.ds(where, 1), q : q + cell_rows] += sums[h : h + 1]

    @pl.when(step == pl.num_programs(0) - 1)
    def _():
        out_ref[...] = (2.0 * total[...]).astype(out_ref.dtype)


def tile_sums(blocks, center, expo, slope, dest, tiles, row_of, row_count, out_type):
    number, width = blocks.shape[0], blocks.shape[1]
    per_step = min(STEP_BLOCKS, number)

    def flat(values):
        return values.reshape(-1, width)

    def whole(values):
        return pl.BlockSpec(values.shape, lambda g: (0, 0))

    tables = (flat(jnp.swapaxes(center, 1, 2)), flat(expo), flat(jnp.swapaxes(slope, 1, 2)))
    scalars = pl.BlockSpec(memory_space=pltpu.SMEM)
    return pl.pallas_call(
        functools.partial(density_kernel, row_of=row_of),
        grid=(number // per_step,),
        in_specs=[
            scalars,
            scalars,
            pl.BlockSpec((per_step, width, width), lambda g: (g, 0, 0)),
            *[whole(values) for values in tables],
        ],
        out_specs=pl.BlockSpec((row_count, CELLS), lambda g: (0, 0)),
        out_shape=jax.ShapeDtypeStruct((row_count, CELLS), out_type),
        scratch_shapes=[
            pltpu.VMEM((per_step // 2, 2 * width, 2 * width), jnp.bfloat16),
            pltpu.VMEM((row_count, CELLS), jnp.float32),
            *[pltpu.VMEM(values.shape, jnp.float32) for values in tables],
            pltpu.VMEM((2 * per_step, (TPB + 2) * TE, width), jnp.float32),
            *[pltpu.VMEM((TPB * CELLS, 2 * width), jnp.bfloat16)] * (per_step // 2),
        ],
        compiler_params=pltpu.CompilerParams(vmem_limit_bytes=60 << 20),
    )(dest.T, tiles.T, blocks, *tables)


def pick_rows(summed, order):
    match = order[:, None] == jnp.arange(summed.shape[0], dtype=jnp.int32)[None, :]
    return jnp.sum(jnp.where(match[:, :, None], summed[None], 0.0), axis=1)


def dense_plan(blocks, center, expo, slope, dest, tiles, order, dom_count, sub_count):
    quarter = TPD // sub_count
    held = dom_count * quarter

    def row_of(dest_ref, tile_ref, block, k):
        tile = tile_ref[k, block]
        return tile // quarter * held + dest_ref[0, block] * quarter + tile % quarter

    partial = tile_sums(
        blocks, center, expo, slope, dest, tiles, row_of, dom_count * sub_count * held, jnp.bfloat16
    )
    moved = lax.all_to_all(
        partial.reshape(dom_count * sub_count, held, CELLS), AXES, split_axis=0, concat_axis=0, tiled=True
    )
    return pick_rows(jnp.sum(moved.astype(jnp.float32), axis=0), order)


def routed_plan(blocks, center, expo, slope, dest, tiles, order, dom_count, sub_count):
    number = blocks.shape[0]
    capacity = max(2, 2 * number // dom_count)
    tile_count = dom_count * TPD
    quarter = TPD // sub_count

    def row_of(dest_ref, tile_ref, block, k):
        return TPB * block + k

    density = tile_sums(
        blocks, center, expo, slope, dest, tiles, row_of, TPB * number, jnp.float32
    )
    density = density.reshape(number, TPB, CELLS).astype(jnp.bfloat16)
    targets = dest[:, 0]
    one_hot = (targets[:, None] == jnp.arange(dom_count, dtype=jnp.int32)[None, :]).astype(jnp.int32)
    places = jnp.sum((jnp.cumsum(one_hot, axis=0) - one_hot) * one_hot, axis=1)

    def exchange(values, filler):
        holder = jnp.full((dom_count, capacity) + values.shape[1:], filler, values.dtype)
        holder = holder.at[targets, places].set(values)
        return lax.all_to_all(holder, "dom", split_axis=0, concat_axis=0, tiled=True)

    arrived = exchange(density, 0).reshape(-1, CELLS).astype(jnp.float32)
    tile_ids = exchange(tiles, tile_count).reshape(-1)
    partial = jnp.zeros((tile_count, CELLS), jnp.float32).at[tile_ids].add(arrived, mode="drop")
    moved = lax.all_to_all(
        partial.reshape(dom_count, TPD, CELLS), "dom", split_axis=0, concat_axis=0, tiled=True
    )
    summed = lax.psum_scatter(moved, "sub", scatter_dimension=1, tiled=True)
    return summed.reshape(dom_count * quarter, CELLS)[order]


def local(blocks, center, expo, slope, dest, tiles, slab_from):
    dom_count, sub_count = lax.axis_size("dom"), lax.axis_size("sub")
    all_rows = dom_count * dom_count * TPD
    plan = dense_plan if all_rows <= DENSE_ROWS else routed_plan
    return plan(blocks, center, expo, slope, dest, tiles, slab_from[0], dom_count, sub_count)


def solution(mesh):
    def placed(rank):
        return P(AXES, *([None] * (rank - 1)))

    return jax.shard_map(
        local,
        mesh=mesh,
        in_specs=tuple(placed(rank) for rank in (3, 4, 3, 4, 2, 2, 2)),
        out_specs=placed(2),
        check_vma=False,
    )
```

time: 42.8 us -> 31.7 us (0.74)
  Pallas kernels: 18.1 us -> 12.8 us
  local copies, waits for them, and re-layouts: 4.34 us -> 0.01 us
  other arithmetic: 2.25 us -> 0.84 us
    pallas_call x1, Pallas kernels: 18.1 us -> 12.8 us  [tile_sums(): pl.pallas_call(functools.partial(density_kernel, row_of=row_of), grid=(nu...]
    unnamed x8 -> x2, local copies, waits for them, and re-layouts: 4.24 us -> 0.01 us
    add x1 -> x0, other arithmetic: 0.73 us -> none  [dense_plan(): rows = tiles // quarter * held + dest * quarter + tiles % quarter]
    mul x1 -> x0, other arithmetic: 0.68 us -> none  [dense_plan(): rows = tiles // quarter * held + dest * quarter + tiles % quarter]
where the time goes in v2:
time: 31.7 us; the launch traced here: 31.5 us
  Pallas kernels  12.8 us (40%)
  waiting for transfers between devices  10.5 us (33%)
  starting transfers between devices  7.3 us (23%)
  other arithmetic  0.84 us (3%)
    pallas_call x1, Pallas kernels, tile_sums(): pl.pallas_call(functools.partial(density_kernel, row_of=row_of), grid=(nu...  12.8 us
    all_to_all x1, waiting for transfers between devices, dense_plan(): lax.all_to_all(partial.reshape(dom_count * sub_count, held, CELLS), AXES,...  10.5 us
    all_to_all x1, starting transfers between devices, dense_plan(): lax.all_to_all(partial.reshape(dom_count * sub_count, held, CELLS), AXES,...  7.3 us
    reduce_sum x1, other arithmetic, pick_rows(): return jnp.sum(jnp.where(match[:, :, None], summed[None], 0.0), axis=1)  0.72 us
  transfers between devices with their start and end apart: 1, of which 1 were waited for; matrix products, arithmetic and copies ran while one was open for 0% of the time, Pallas kernels for 0%

profile of v2, /device:TPU:0, one launch (start us, length us, event | category | flops | bytes accessed | tf_op | source)
XLA Modules:
  0.0 31.5 jit_solution(505334085952421552)
XLA Ops:
  0.0 0.0 copy-start
  0.0 12.8 %shard_map.73 = bf16[256,512]{1,0:T(8,128)(2,1)} custom-call(s32[1,64]{1,0:T(1,128)} %bitcast.16, s32[2,64]{1,0:T(2,128)} %bitcast.15, bf16[64,128,128]{2,1,0:T(8,128)(2,1)} %blocks_ref.1, bf16[384,128]{1,0:T(8,128)(2,1)} %bitcast.12, bf16[128,128]{1,0:T(8,128)(2,1)} %bitcast.14, bf16[384,128]{1,0:T(8,128)(2,1)} %bitcast.13), custom_call_target="tpu_custom_call" | custom-call | tf_op jit(solution)/shard_map/pallas_call | solution.py:154
  12.8 7.3 %all-to-all-start = ((bf16[32,8,512]{2,1,0:T(8,128)(2,1)}), bf16[32,8,512]{2,1,0:T(8,128)(2,1)S(1)}, u32[]{:S(2)}, u32[]{:S(2)}) async-start(bf16[32,8,512]{2,1,0:T(8,128)(2,1)} %bitcast.11), calls=%async_computation | async-start | bytes 524288 | tf_op jit(solution)/shard_map/all_to_all | solution.py:192
  20.1 0.0 copy-done
  20.1 0.1 iota_compare_fusion
  20.2 10.5 %all-to-all-done = bf16[32,8,512]{2,1,0:T(8,128)(2,1)S(1)} async-done(((bf16[32,8,512]{2,1,0:T(8,128)(2,1)}), bf16[32,8,512]{2,1,0:T(8,128)(2,1)S(1)}, u32[]{:S(2)}, u32[]{:S(2)}) %all-to-all-start) | async-done | bytes 262176 | tf_op jit(solution)/shard_map/all_to_all | solution.py:192
  30.8 0.7 %select_reduce_fusion = f32[8,512]{1,0:T(8,128)} fusion(f32[8,512]{1,0:T(8,128)S(1)} %convert_reduce_fusion, pred[8,8]{1,0:T(8,128)(4,1)S(1)} %iota_compare_fusion), kind=kLoop, calls=%fused_computation.1 | loop fusion | flops 61440 | bytes 32832 | tf_op jit(solution)/shard_map/reduce_sum | solution.py:178
  (1 shorter events, 0.0 us)
Async XLA Ops:
  0.0 20.1 %copy-start = (s32[1,8]{1,0:T(1,128)S(1)}, s32[1,8]{1,0:T(1,128)}, u32[]{:S(2)}) copy-start(s32[1,8]{1,0:T(1,128)} %param.13) | copy-start | bytes 100
  12.8 17.9 %all-to-all-start = ((bf16[32,8,512]{2,1,0:T(8,128)(2,1)}), bf16[32,8,512]{2,1,0:T(8,128)(2,1)S(1)}, u32[]{:S(2)}, u32[]{:S(2)}) async-start(bf16[32,8,512]{2,1,0:T(8,128)(2,1)} %bitcast.11), calls=%async_computation | async-start | bytes 524288 | tf_op jit(solution)/shard_map/all_to_all | solution.py:192

commit v3 on v2

--- a/solution.py
+++ b/solution.py
@@ -13,7 +13,7 @@
 CELLS = TE**3
 PLANE = TE * TE
 AXES = ("dom", "sub")
-STEP_BLOCKS = 16
+STEP_BLOCKS = 32
 LOG2_E = 1.4426950408889634
 DENSE_ROWS = 1024
 
@@ -51,7 +51,6 @@
     expo_ref,
     slope_ref,
     out_ref,
-    weight,
     total,
     centers,
     expos,
@@ -62,11 +61,10 @@
 ):
     step = pl.program_id(0)
     count, width = blocks_ref.shape[0], blocks_ref.shape[1]
-    cell_rows = 4 * PLANE
+    part_rows = 4 * PLANE
 
     @pl.when(step == 0)
     def _():
-        weight[...] = jnp.zeros_like(weight)
         total[...] = jnp.zeros_like(total)
         centers[...] = center_ref[...].astype(jnp.float32)
         expos[...] = expo_ref[...].astype(jnp.float32)
@@ -83,56 +81,33 @@
             tables.at[slot],
         )
 
-    pick = lax.broadcasted_iota(jnp.int32, (16, 2 * width), 1) // width
-    pick = (pick == lax.broadcasted_iota(jnp.int32, (16, 2 * width), 0)).astype(jnp.float32)
-    pick = pick.astype(jnp.bfloat16)
+    ones = jnp.ones((16, width), jnp.bfloat16)
     transposed = (((1,), (1,)), ((), ()))
-    half_points = TPB * CELLS // 2
-
-    for pair in range(count // 2):
-        column = columns[pair]
-        first = step * count + 2 * pair
-        for h in range(2):
-            own = slice(h * width, (h + 1) * width)
-            weight[pair, own, own] = blocks_ref[2 * pair + h]
-            row, t, d = factors(first + h, 1, 4 * pair + h)
-            for x in range(TPB * TE):
+
+    for i in range(count):
+        block = step * count + i
+        column = columns[i]
+        row, t, d = factors(block, 1, 2 * i)
+        for x in range(TPB * TE):
+            value = (t * row(x)[None]).reshape(PLANE, width)
+            column[x * PLANE : (x + 1) * PLANE, :] = value.astype(jnp.bfloat16)
+            t = t + d
+        product = lax.dot_general(
+            column[...], blocks_ref[i], transposed, preferred_element_type=jnp.float32
+        )
+        row, t, d = factors(block, 0, 2 * i + 1)
+        for part in range(TPB * CELLS // part_rows):
+            planes = []
+            for x in range(4 * part, 4 * part + 4):
                 value = (t * row(x)[None]).reshape(PLANE, width)
-                column[x * PLANE : (x + 1) * PLANE, own] = value.astype(jnp.bfloat16)
+                value = value * product[x * PLANE : (x + 1) * PLANE, :]
+                planes.append(value.astype(jnp.bfloat16))
                 t = t + d
-        sides = [list(factors(first + h, 0, 4 * pair + 2 + h)) for h in range(2)]
-        for half in range(2):
-            product = lax.dot_general(
-                column[half * half_points : (half + 1) * half_points, :],
-                weight[pair],
-                transposed,
-                preferred_element_type=jnp.float32,
-            )
-            for part in range(half_points // cell_rows):
-                scaled = []
-                for h in range(2):
-                    row, t, d = sides[h]
-                    planes = []
-                    for plane in range(4):
-                        at = part * cell_rows + plane * PLANE
-                        x = half * (half_points // PLANE) + part * 4 + plane
-                        value = (t * row(x)[None]).reshape(PLANE, width)
-                        value = value * product[at : at + PLANE, h * width : (h + 1) * width]
-                        planes.append(value.astype(jnp.bfloat16))
-                        t = t + d
-                    sides[h][1] = t
-                    scaled.append(jnp.concatenate(planes, axis=0))
-                sums = lax.dot_general(
-                    pick,
-                    jnp.concatenate(scaled, axis=1),
-                    transposed,
-                    preferred_element_type=jnp.float32,
-                )
-                start = half * half_points + part * cell_rows
-                k, q = start // CELLS, start % CELLS
-                for h in range(2):
-                    where = row_of(dest_ref, tile_ref, first + h, k)
-                    total[pl.ds(where, 1), q : q + cell_rows] += sums[h : h + 1]
+            scaled = jnp.concatenate(planes, axis=0)
+            sums = lax.dot_general(ones, scaled, transposed, preferred_element_type=jnp.float32)
+            k, q = divmod(part * part_rows, CELLS)
+            where = row_of(dest_ref, tile_ref, block, k)
+            total[pl.ds(where, 1), q : q + part_rows] += sums[0:1]
 
     @pl.when(step == pl.num_programs(0) - 1)
     def _():
@@ -163,11 +138,10 @@
         out_specs=pl.BlockSpec((row_count, CELLS), lambda g: (0, 0)),
         out_shape=jax.ShapeDtypeStruct((row_count, CELLS), out_type),
         scratch_shapes=[
-            pltpu.VMEM((per_step // 2, 2 * width, 2 * width), jnp.bfloat16),
             pltpu.VMEM((row_count, CELLS), jnp.float32),
             *[pltpu.VMEM(values.shape, jnp.float32) for values in tables],
             pltpu.VMEM((2 * per_step, (TPB + 2) * TE, width), jnp.float32),
-            *[pltpu.VMEM((TPB * CELLS, 2 * width), jnp.bfloat16)] * (per_step // 2),
+            *[pltpu.VMEM((TPB * CELLS, width), jnp.bfloat16)] * per_step,
         ],
         compiler_params=pltpu.CompilerParams(vmem_limit_bytes=60 << 20),
     )(dest.T, tiles.T, blocks, *tables)

time: 31.7 us -> 30.6 us (0.965)
  Pallas kernels: 12.8 us -> 11.7 us
    pallas_call x1, Pallas kernels: 12.8 us -> 11.7 us  [tile_sums(): pl.pallas_call(functools.partial(density_kernel, row_of=row_of), grid=(nu...]
where the time goes in v3:
time: 30.6 us; the launch traced here: 30.3 us
  Pallas kernels  11.7 us (38%)
  waiting for transfers between devices  10.5 us (34%)
  starting transfers between devices  7.3 us (24%)
  other arithmetic  0.84 us (3%)
    pallas_call x1, Pallas kernels, tile_sums(): pl.pallas_call(functools.partial(density_kernel, row_of=row_of), grid=(nu...  11.7 us
    all_to_all x1, waiting for transfers between devices, dense_plan(): lax.all_to_all(partial.reshape(dom_count * sub_count, held, CELLS), AXES,...  10.5 us
    all_to_all x1, starting transfers between devices, dense_plan(): lax.all_to_all(partial.reshape(dom_count * sub_count, held, CELLS), AXES,...  7.3 us
    reduce_sum x1, other arithmetic, pick_rows(): return jnp.sum(jnp.where(match[:, :, None], summed[None], 0.0), axis=1)  0.72 us
  transfers between devices with their start and end apart: 1, of which 1 were waited for; matrix products, arithmetic and copies ran while one was open for 0% of the time, Pallas kernels for 0%

profile of v3, /device:TPU:0, one launch (start us, length us, event | category | flops | bytes accessed | tf_op | source)
XLA Modules:
  0.0 30.3 jit_solution(15267275655579843080)
XLA Ops:
  0.0 0.0 copy-start
  0.0 11.7 %shard_map.73 = bf16[256,512]{1,0:T(8,128)(2,1)} custom-call(s32[1,64]{1,0:T(1,128)} %bitcast.16, s32[2,64]{1,0:T(2,128)} %bitcast.15, bf16[64,128,128]{2,1,0:T(8,128)(2,1)} %blocks_ref.1, bf16[384,128]{1,0:T(8,128)(2,1)} %bitcast.12, bf16[128,128]{1,0:T(8,128)(2,1)} %bitcast.14, bf16[384,128]{1,0:T(8,128)(2,1)} %bitcast.13), custom_call_target="tpu_custom_call" | custom-call | tf_op jit(solution)/shard_map/pallas_call | solution.py:129
  11.7 7.3 %all-to-all-start = ((bf16[32,8,512]{2,1,0:T(8,128)(2,1)}), bf16[32,8,512]{2,1,0:T(8,128)(2,1)S(1)}, u32[]{:S(2)}, u32[]{:S(2)}) async-start(bf16[32,8,512]{2,1,0:T(8,128)(2,1)} %bitcast.11), calls=%async_computation | async-start | bytes 524288 | tf_op jit(solution)/shard_map/all_to_all | solution.py:166
  19.0 0.0 copy-done
  19.0 0.1 iota_compare_fusion
  19.1 10.5 %all-to-all-done = bf16[32,8,512]{2,1,0:T(8,128)(2,1)S(1)} async-done(((bf16[32,8,512]{2,1,0:T(8,128)(2,1)}), bf16[32,8,512]{2,1,0:T(8,128)(2,1)S(1)}, u32[]{:S(2)}, u32[]{:S(2)}) %all-to-all-start) | async-done | bytes 262176 | tf_op jit(solution)/shard_map/all_to_all | solution.py:166
  29.6 0.7 %select_reduce_fusion = f32[8,512]{1,0:T(8,128)} fusion(f32[8,512]{1,0:T(8,128)S(1)} %convert_reduce_fusion, pred[8,8]{1,0:T(8,128)(4,1)S(1)} %iota_compare_fusion), kind=kLoop, calls=%fused_computation.1 | loop fusion | flops 61440 | bytes 32832 | tf_op jit(solution)/shard_map/reduce_sum | solution.py:152
  (1 shorter events, 0.0 us)
Async XLA Ops:
  0.0 19.0 %copy-start = (s32[1,8]{1,0:T(1,128)S(1)}, s32[1,8]{1,0:T(1,128)}, u32[]{:S(2)}) copy-start(s32[1,8]{1,0:T(1,128)} %param.13) | copy-start | bytes 100
  11.7 17.9 %all-to-all-start = ((bf16[32,8,512]{2,1,0:T(8,128)(2,1)}), bf16[32,8,512]{2,1,0:T(8,128)(2,1)S(1)}, u32[]{:S(2)}, u32[]{:S(2)}) async-start(bf16[32,8,512]{2,1,0:T(8,128)(2,1)} %bitcast.11), calls=%async_computation | async-start | bytes 524288 | tf_op jit(solution)/shard_map/all_to_all | solution.py:166

commit v4 on v3

--- a/solution.py
+++ b/solution.py
@@ -56,7 +56,7 @@
     expos,
     slopes,
     tables,
-    *columns,
+    *,
     row_of,
 ):
     step = pl.program_id(0)
@@ -86,14 +86,15 @@
 
     for i in range(count):
         block = step * count + i
-        column = columns[i]
         row, t, d = factors(block, 1, 2 * i)
+        planes = []
         for x in range(TPB * TE):
             value = (t * row(x)[None]).reshape(PLANE, width)
-            column[x * PLANE : (x + 1) * PLANE, :] = value.astype(jnp.bfloat16)
+            planes.append(value.astype(jnp.bfloat16))
             t = t + d
+        column = jnp.concatenate(planes, axis=0)
         product = lax.dot_general(
-            column[...], blocks_ref[i], transposed, preferred_element_type=jnp.float32
+            column, blocks_ref[i], transposed, preferred_element_type=jnp.float32
         )
         row, t, d = factors(block, 0, 2 * i + 1)
         for part in range(TPB * CELLS // part_rows):
@@ -141,7 +142,6 @@
             pltpu.VMEM((row_count, CELLS), jnp.float32),
             *[pltpu.VMEM(values.shape, jnp.float32) for values in tables],
             pltpu.VMEM((2 * per_step, (TPB + 2) * TE, width), jnp.float32),
-            *[pltpu.VMEM((TPB * CELLS, width), jnp.bfloat16)] * per_step,
         ],
         compiler_params=pltpu.CompilerParams(vmem_limit_bytes=60 << 20),
     )(dest.T, tiles.T, blocks, *tables)

time: 30.6 us -> 30.5 us (level)
  no operation moved by 1% of the time
where the time goes in v4:
time: 30.5 us; the launch traced here: 30.3 us
  Pallas kernels  11.6 us (38%)
  waiting for transfers between devices  10.5 us (34%)
  starting transfers between devices  7.3 us (24%)
  other arithmetic  0.84 us (3%)
    pallas_call x1, Pallas kernels, tile_sums(): pl.pallas_call(functools.partial(density_kernel, row_of=row_of), grid=(nu...  11.6 us
    all_to_all x1, waiting for transfers between devices, dense_plan(): lax.all_to_all(partial.reshape(dom_count * sub_count, held, CELLS), AXES,...  10.5 us
    all_to_all x1, starting transfers between devices, dense_plan(): lax.all_to_all(partial.reshape(dom_count * sub_count, held, CELLS), AXES,...  7.3 us
    reduce_sum x1, other arithmetic, pick_rows(): return jnp.sum(jnp.where(match[:, :, None], summed[None], 0.0), axis=1)  0.72 us
  transfers between devices with their start and end apart: 1, of which 1 were waited for; matrix products, arithmetic and copies ran while one was open for 0% of the time, Pallas kernels for 0%

profile of v4, /device:TPU:0, one launch (start us, length us, event | category | flops | bytes accessed | tf_op | source)
XLA Modules:
  0.0 30.3 jit_solution(15555532149608870506)
XLA Ops:
  0.0 0.0 copy-start
  0.0 11.6 %shard_map.73 = bf16[256,512]{1,0:T(8,128)(2,1)} custom-call(s32[1,64]{1,0:T(1,128)} %bitcast.16, s32[2,64]{1,0:T(2,128)} %bitcast.15, bf16[64,128,128]{2,1,0:T(8,128)(2,1)} %blocks_ref.1, bf16[384,128]{1,0:T(8,128)(2,1)} %bitcast.12, bf16[128,128]{1,0:T(8,128)(2,1)} %bitcast.14, bf16[384,128]{1,0:T(8,128)(2,1)} %bitcast.13), custom_call_target="tpu_custom_call" | custom-call | tf_op jit(solution)/shard_map/pallas_call | solution.py:130
  11.6 7.3 %all-to-all-start = ((bf16[32,8,512]{2,1,0:T(8,128)(2,1)}), bf16[32,8,512]{2,1,0:T(8,128)(2,1)S(1)}, u32[]{:S(2)}, u32[]{:S(2)}) async-start(bf16[32,8,512]{2,1,0:T(8,128)(2,1)} %bitcast.11), calls=%async_computation | async-start | bytes 524288 | tf_op jit(solution)/shard_map/all_to_all | solution.py:166
  18.9 0.0 copy-done
  18.9 0.1 iota_compare_fusion
  19.0 10.5 %all-to-all-done = bf16[32,8,512]{2,1,0:T(8,128)(2,1)S(1)} async-done(((bf16[32,8,512]{2,1,0:T(8,128)(2,1)}), bf16[32,8,512]{2,1,0:T(8,128)(2,1)S(1)}, u32[]{:S(2)}, u32[]{:S(2)}) %all-to-all-start) | async-done | bytes 262176 | tf_op jit(solution)/shard_map/all_to_all | solution.py:166
  29.6 0.7 %select_reduce_fusion = f32[8,512]{1,0:T(8,128)} fusion(f32[8,512]{1,0:T(8,128)S(1)} %convert_reduce_fusion, pred[8,8]{1,0:T(8,128)(4,1)S(1)} %iota_compare_fusion), kind=kLoop, calls=%fused_computation.1 | loop fusion | flops 61440 | bytes 32832 | tf_op jit(solution)/shard_map/reduce_sum | solution.py:152
  (1 shorter events, 0.0 us)
Async XLA Ops:
  0.0 18.9 %copy-start = (s32[1,8]{1,0:T(1,128)S(1)}, s32[1,8]{1,0:T(1,128)}, u32[]{:S(2)}) copy-start(s32[1,8]{1,0:T(1,128)} %param.13) | copy-start | bytes 100
  11.6 17.9 %all-to-all-start = ((bf16[32,8,512]{2,1,0:T(8,128)(2,1)}), bf16[32,8,512]{2,1,0:T(8,128)(2,1)S(1)}, u32[]{:S(2)}, u32[]{:S(2)}) async-start(bf16[32,8,512]{2,1,0:T(8,128)(2,1)} %bitcast.11), calls=%async_computation | async-start | bytes 524288 | tf_op jit(solution)/shard_map/all_to_all | solution.py:166
